TPU v7x, 256 devices: a whole 4x4x8 slice. The times are simulated.
256 devices in a mesh: group: 8 (over z_lo, y), dev: 32 (over z_hi, x, core).
Axes of the slice: x: 4, y: 4, z: 8 (z_hi: 4, z_lo: 2; z = z_hi * 2 + z_lo), core: 2. Of those that a mesh axis runs over, the one named last changes fastest.
Arguments:
- tiles: bfloat16 [256, 256, 1280], P(('group', 'dev')), may hold values from -6 to 6
- w_qkv: bfloat16 [1280, 3840], P('dev'), may hold values from -0.15625 to 0.15625
- w_out: bfloat16 [1280, 1280], replicated, may hold values from -0.15625 to 0.15625
- w_kv: bfloat16 [1280, 1024], replicated, may hold values from -0.15625 to 0.15625
- ln_gain: float32 [1280], replicated, may hold values from 0.25 to 1.75
- ln_bias: float32 [1280], replicated, may hold values from -2 to 2
- k_gain: float32 [128], replicated, may hold values from 0.5 to 2
- cross_queries: bfloat16 [16384, 4096], P(('group', 'dev')), may hold values from -110 to 110
- self_queries: bfloat16 [16384, 4096], P(('group', 'dev')), may hold values from -110 to 110
- text_kv: bfloat16 [16384, 1024], P(('group', 'dev')), may hold values from -6 to 6
- tiles_per_image: int32 [8, 16], replicated, may hold values from 1 to 4, 32 in all within a row
- request_table: int32 [8, 2], replicated, may hold values from 0 to 127
- span_offsets: int32 [8], replicated, may hold values from 0 to 2047
Outputs:
- cross_context: bfloat16 [16384, 4096], P(('group', 'dev'))
- self_context: bfloat16 [16384, 4096], P(('group', 'dev'))
Inputs may be any that keep to these rules, and one draw needn't show every extreme that they name: `tiles_per_image`: each row sums to 32; some image has exactly 4 tiles.
All inputs are finite; a program needn't handle non-finite values.
Results may differ from a plain program's by a relative error of at most 0.03.
Values may be sent and summed in bfloat16 or wider, within the bound.
No kernel may reach another device: no remote copies, remote signals or barrier semaphores. Data moves between devices by JAX's collectives and lax.ppermute only.
A program may use at most 64 MiB of HBM per device.

v0:
```python
import math

import jax
import jax.numpy as jnp
from jax import lax
from jax.sharding import PartitionSpec as P

VH = 16
VHD = 80
HQ = 32
KVH = 4
HD = 128
SLOTS = 2
MAXT = 4


def layer_norm(values, gain, bias):
    widened = values.astype(jnp.float32)
    center = jnp.mean(widened, axis=-1, keepdims=True)
    spread = jnp.mean(jnp.square(widened - center), axis=-1, keepdims=True)
    return ((widened - center) * lax.rsqrt(spread + 1e-05) * gain + bias).astype(jnp.bfloat16)


def tile_attention(qkv_out):
    row_count = qkv_out.shape[0]
    sections = qkv_out.reshape(row_count, 3, VH, VHD)
    scores = jnp.einsum(
        "qhd,khd->hqk", sections[:, 0], sections[:, 1], preferred_element_type=jnp.float32
    ) / math.sqrt(VHD)
    highest = jnp.max(scores, axis=-1, keepdims=True)
    exponent = jnp.exp(scores - highest)
    weights = (exponent / jnp.sum(exponent, axis=-1, keepdims=True)).astype(jnp.bfloat16)
    context = jnp.einsum(
        "hqk,khd->qhd", weights, sections[:, 2], preferred_element_type=jnp.float32
    )
    return context.reshape(row_count, VH * VHD).astype(jnp.bfloat16)


def finish_tile(tile_rows, context, w_out, w_kv, k_gain):
    residual_sum = (
        tile_rows.astype(jnp.float32) + jnp.dot(context, w_out, preferred_element_type=jnp.float32)
    ).astype(jnp.bfloat16)
    projected = jnp.dot(residual_sum, w_kv, preferred_element_type=jnp.float32)
    row_count = projected.shape[0]
    key_part = projected[:, : KVH * HD].reshape(row_count, KVH, HD)
    key_part = (
        key_part
        * lax.rsqrt(jnp.mean(jnp.square(key_part), axis=-1, keepdims=True) + 1e-06)
        * k_gain
    )
    return jnp.concatenate(
        [key_part.reshape(row_count, KVH * HD), projected[:, KVH * HD :]], axis=1
    ).astype(jnp.bfloat16)


def attend(queries, keyvals, key_mask):
    row_count = queries.shape[0]
    key_count = keyvals.shape[0]
    group_size = HQ // KVH
    query_part = queries.reshape(row_count, KVH, group_size, HD).transpose(1, 0, 2, 3)
    key_part = keyvals[:, : KVH * HD].reshape(key_count, KVH, HD).transpose(1, 0, 2)
    value_part = keyvals[:, KVH * HD :].reshape(key_count, KVH, HD).transpose(1, 0, 2)

    def one_head(operand):
        query_head, key_head, value_head = operand
        scores = jnp.einsum(
            "rgd,kd->grk", query_head, key_head, preferred_element_type=jnp.float32
        ) / math.sqrt(HD)
        highest = jnp.max(jnp.where(key_mask, scores, -jnp.inf), axis=-1, keepdims=True)
        exponent = jnp.where(key_mask, jnp.exp(scores - highest), 0.0)
        weights = (exponent / jnp.sum(exponent, axis=-1, keepdims=True)).astype(jnp.bfloat16)
        return jnp.einsum("grk,kd->rgd", weights, value_head, preferred_element_type=jnp.float32)

    outputs = lax.map(one_head, (query_part, key_part, value_part))
    return outputs.transpose(1, 0, 2, 3).reshape(row_count, HQ * HD).astype(jnp.bfloat16)


def per_device(
    tiles,
    w_qkv,
    w_out,
    w_kv,
    ln_gain,
    ln_bias,
    k_gain,
    cross_queries,
    self_queries,
    text_kv,
    tiles_per_image,
    request_table,
    span_offsets,
):
    tiles_dev, row_count, feature = tiles.shape
    flat_rows = tiles.reshape(tiles_dev * row_count, feature)
    normed = layer_norm(flat_rows, ln_gain, ln_bias)
    qkv_out = jnp.dot(
        normed, lax.all_gather(w_qkv, "dev", axis=0, tiled=True), preferred_element_type=jnp.float32
    ).astype(jnp.bfloat16)
    context = lax.map(tile_attention, qkv_out.reshape(tiles_dev, row_count, w_qkv.shape[1]))
    kv_rows = finish_tile(
        flat_rows, context.reshape(tiles_dev * row_count, feature), w_out, w_kv, k_gain
    )
    dev_count = lax.axis_size("dev")
    group_count = lax.axis_size("group")
    row_block = row_count // dev_count
    channels = kv_rows.shape[1]
    blocks = lax.all_to_all(
        kv_rows.reshape(tiles_dev, dev_count, row_block, channels),
        "dev",
        split_axis=1,
        concat_axis=0,
        tiled=True,
    )
    tiles_group = tiles_dev * dev_count
    blocks = blocks.reshape(tiles_group, row_block * channels)
    images_group = tiles_per_image.shape[1]
    flat_tiles = tiles_per_image.reshape(-1)
    starts = (jnp.cumsum(tiles_per_image, axis=1) - tiles_per_image).reshape(-1)
    catalog = jnp.arange(flat_tiles.shape[0], dtype=jnp.int32)
    matches = request_table[:, :, None] == catalog[None, None, :]
    counts = jnp.sum(jnp.where(matches, flat_tiles[None, None, :], 0), axis=-1)
    first_tile = jnp.sum(jnp.where(matches, starts[None, None, :], 0), axis=-1)
    owner_group = request_table // images_group
    tile_step = jnp.arange(MAXT, dtype=jnp.int32)
    positions = request_table.shape[1] * MAXT
    is_valid = (tile_step[None, None, :] < counts[:, :, None]).reshape(group_count, positions)
    global_tile = (
        owner_group[:, :, None] * tiles_group + first_tile[:, :, None] + tile_step[None, None, :]
    ).reshape(group_count, positions)
    group_id = lax.axis_index("group")
    mine_valid = lax.dynamic_index_in_dim(is_valid, group_id, 0, keepdims=False)
    gathered = lax.all_gather(blocks, "group", axis=0, tiled=True)
    mine_tile = lax.dynamic_index_in_dim(global_tile, group_id, 0, keepdims=False)
    every_tile = jnp.arange(group_count * tiles_group, dtype=jnp.int32)
    onehot = ((mine_tile[:, None] == every_tile[None, :]) & mine_valid[:, None]).astype(
        jnp.bfloat16
    )
    picked = jnp.dot(onehot, gathered, preferred_element_type=jnp.float32).astype(jnp.bfloat16)
    picked = picked.reshape(positions, row_block, channels)
    image_kv = lax.all_gather(picked, "dev", axis=1, tiled=True).reshape(
        positions * row_count, channels
    )
    text_all = lax.all_gather(text_kv, "dev", axis=0, tiled=True)
    tok_rows = cross_queries.shape[0]
    span_len = tok_rows * dev_count
    local_row = lax.axis_index("dev") * tok_rows + jnp.arange(tok_rows, dtype=jnp.int32)
    offset = lax.dynamic_index_in_dim(span_offsets, group_id, 0, keepdims=False)
    position = offset + local_row
    slot_index = jnp.arange(positions, dtype=jnp.int32) // MAXT
    visible = (position[:, None] >= slot_index[None, :] * (span_len // SLOTS)) & mine_valid[None, :]
    key_mask = jnp.repeat(visible, row_count, axis=1)
    cross_out = attend(cross_queries, image_kv, key_mask)
    causal = local_row[:, None] >= jnp.arange(span_len, dtype=jnp.int32)[None, :]
    self_out = attend(self_queries, text_all, causal)
    return (cross_out, self_out)


def solution(mesh):
    in_specs = (
        P(("group", "dev"), None, None),
        P("dev", None),
        P(),
        P(),
        P(),
        P(),
        P(),
        P(("group", "dev"), None),
        P(("group", "dev"), None),
        P(("group", "dev"), None),
        P(),
        P(),
        P(),
    )
    out_specs = (P(("group", "dev"), None), P(("group", "dev"), None))
    return jax.shard_map(
        per_device, mesh=mesh, in_specs=in_specs, out_specs=out_specs, check_vma=False
    )
```

profile of v0, /device:TPU:1, one launch (start us, length us, event | category | flops | bytes accessed | tf_op | source)
XLA Modules:
  0.0 385.3 jit_solution(2816763021480834178)
XLA Ops:
  11.5 89.5 %all-gather.5.cloned.1.call-done = bf16[1280,3840]{1,0:T(8,128)(2,1)} async-done(((bf16[40,3840]{1,0:T(8,128)(2,1)}), bf16[1280,3840]{1,0:T(8,128)(2,1)}) %all-gather.5.cloned.1.call-update) | async-done | bytes 9830416 | tf_op jit(solution)/shard_map/all_gather | solution.py:97
  101.0 8.2 %convolution_convert_fusion.1 = bf16[256,3840]{1,0:T(8,128)(2,1)} fusion(bf16[1280,3840]{1,0:T(8,128)(2,1)} %all-gather.5.cloned.1.call-done, bf16[1,256,1280]{2,1,0:T(8,128)(2,1)} %param.17, f32[1280]{0:T(1024)} %param.22, f32[1280]{0:T(1024)} %param.21, f32[256]{0:T(256)S(1)} %add_rsqrt_fusion.1, f32[256]{0:T(256)S(1)} %broadcast_multiply_fusion), kind=kOutput, calls=%fused_computation.63 | convolution fusion | flops 2519531520 | bytes 12464128 | tf_op jit(solution)/shard_map/dot_general | solution.py:96
  109.2 4.0 %copy.90 = bf16[256,3840]{0,1:T(8,128)(2,1)} copy(bf16[256,3840]{1,0:T(8,128)(2,1)} %convolution_convert_fusion.1) | data formatting | bytes 3932160 | tf_op jit(solution)/shard_map/convert_element_type | solution.py:98
  115.2 3.1 fusion.114
  120.8 4.9 %fusion.85 = f32[256,1024]{1,0:T(8,128)} fusion(bf16[1280,1024]{1,0:T(8,128)(2,1)} %param.20, bf16[256,1280]{0,1:T(8,128)(2,1)} %bitcast.263, bf16[1280,1280]{1,0:T(8,128)(2,1)S(1)} %copy-done, bf16[1,256,1280]{2,1,0:T(8,128)(2,1)} %param.17), kind=kOutput, calls=%fused_computation.82 | convolution fusion | flops 1510932480 | bytes 8257536 | tf_op jit(solution)/shard_map/dot_general | solution.py:43
  129.1 24.6 %all_to_all.4 = bf16[1,32,8,1024]{3,2,0,1:T(8,128)(2,1)S(1)} all-to-all(bf16[1,32,8,1024]{3,2,0,1:T(8,128)(2,1)S(1)} %pad_maximum_fusion), channel_id=1, replica_groups=mesh['group'=8,'dev'=32] {'dev'}, dimensions={1} | all-to-all | bytes 1048576 | tf_op jit(solution)/shard_map/all_to_all | solution.py:107
  157.0 49.1 %all-gather.7.cloned.1.call-done = bf16[256,8192]{1,0:T(8,128)(2,1)} async-done(((bf16[32,8192]{1,0:T(8,128)(2,1)}), bf16[256,8192]{1,0:T(8,128)(2,1)}) %all-gather.7.cloned.1.call-update) | async-done | bytes 4194320 | tf_op jit(solution)/shard_map/all_gather | solution.py:132
  206.1 2.9 convolution_convert_fusion
  211.3 57.0 %all-gather.11.cloned.1.call-done = bf16[2048,1024]{1,0:T(8,128)(2,1)} async-done(((bf16[64,1024]{1,0:T(8,128)(2,1)}), bf16[2048,1024]{1,0:T(8,128)(2,1)}) %all-gather.11.cloned.1.call-update) | async-done | bytes 4194320 | tf_op jit(solution)/shard_map/all_gather | solution.py:143
  268.2 3.8 fusion.112
  272.0 4.0 %copy.116 = bf16[2048,512]{0,1:T(8,128)(2,1)} copy(bf16[2048,512]{1,0:T(8,128)(2,1)} %get-tuple-element.198) | data formatting | bytes 4194304
  278.5 33.3 %while.27 = (s32[]{:T(128)}, bf16[4,64,8,128]{3,1,2,0:T(8,128)(2,1)S(1)}, bf16[4,2048,128]{1,2,0:T(8,128)(2,1)}, bf16[4,2048,128]{1,2,0:T(8,128)(2,1)}, bf16[4,6...) while((s32[]{:T(128)}, bf16[4,64,8,128]{3,1,2,0:T(8,128)(2,1)S(1)}, ...), condition=%wide.region_15.16_spmd.clone, body=%wide.region_12.15_spmd.clone.sunk | while | flops 813828096 | bytes 11149649 | solution.py:74
  278.7 5.0 %fusion.138 = (f32[8,64]{1,0:T(8,128)S(1)}, f32[8,64,2048]{2,1,0:T(8,128)}) fusion(pred[64,2048]{1,0:T(8,128)(4,1)S(1)} %iota_compare_fusion.4, bf16[4,2048,128]{1,2,0:T(8,128)(2,1)} %get-tuple-element.325, s32[]{:T(128)} %get-tuple-element.315, bf16[1,64,8,128]{3,2,0,1:T(8,128)(2,1)S(1)} %constant_dynamic-slice_fusion.5), kind=kOutput, calls=%fused_computation.133.clone.1 | convolution fusion | flops 543164416 | bytes 5770240 | tf_op jit(solution)/shard_map/while/body/eval_jaxpr/sub | solution.py:70
  283.7 3.2 fusion.139
  287.1 5.0 %fusion.138 = (f32[8,64]{1,0:T(8,128)S(1)}, f32[8,64,2048]{2,1,0:T(8,128)}) fusion(pred[64,2048]{1,0:T(8,128)(4,1)S(1)} %iota_compare_fusion.4, bf16[4,2048,128]{1,2,0:T(8,128)(2,1)} %get-tuple-element.325, s32[]{:T(128)} %get-tuple-element.315, bf16[1,64,8,128]{3,2,0,1:T(8,128)(2,1)S(1)} %constant_dynamic-slice_fusion.5), kind=kOutput, calls=%fused_computation.133.clone.1 | convolution fusion | flops 543164416 | bytes 5770240 | tf_op jit(solution)/shard_map/while/body/eval_jaxpr/sub | solution.py:70
  292.0 3.2 fusion.139
  295.4 5.0 %fusion.138 = (f32[8,64]{1,0:T(8,128)S(1)}, f32[8,64,2048]{2,1,0:T(8,128)}) fusion(pred[64,2048]{1,0:T(8,128)(4,1)S(1)} %iota_compare_fusion.4, bf16[4,2048,128]{1,2,0:T(8,128)(2,1)} %get-tuple-element.325, s32[]{:T(128)} %get-tuple-element.315, bf16[1,64,8,128]{3,2,0,1:T(8,128)(2,1)S(1)} %constant_dynamic-slice_fusion.5), kind=kOutput, calls=%fused_computation.133.clone.1 | convolution fusion | flops 543164416 | bytes 5770240 | tf_op jit(solution)/shard_map/while/body/eval_jaxpr/sub | solution.py:70
  300.4 3.2 fusion.139
  303.7 5.0 %fusion.138 = (f32[8,64]{1,0:T(8,128)S(1)}, f32[8,64,2048]{2,1,0:T(8,128)}) fusion(pred[64,2048]{1,0:T(8,128)(4,1)S(1)} %iota_compare_fusion.4, bf16[4,2048,128]{1,2,0:T(8,128)(2,1)} %get-tuple-element.325, s32[]{:T(128)} %get-tuple-element.315, bf16[1,64,8,128]{3,2,0,1:T(8,128)(2,1)S(1)} %constant_dynamic-slice_fusion.5), kind=kOutput, calls=%fused_computation.133.clone.1 | convolution fusion | flops 543164416 | bytes 5770240 | tf_op jit(solution)/shard_map/while/body/eval_jaxpr/sub | solution.py:70
  308.7 3.2 fusion.139
  313.2 16.0 %all-gather.9.cloned.1.call-done = bf16[8,256,1024]{2,1,0:T(8,128)(2,1)} async-done(((bf16[8,8,1024]{2,1,0:T(8,128)(2,1)}), bf16[8,256,1024]{2,1,0:T(8,128)(2,1)}) %all-gather.9.cloned.1.call-update) | async-done | bytes 4194320 | tf_op jit(solution)/shard_map/all_gather | solution.py:140
  329.2 3.8 fusion.113
  333.0 3.9 %copy.97 = bf16[2048,512]{0,1:T(8,128)(2,1)} copy(bf16[2048,512]{1,0:T(8,128)(2,1)} %get-tuple-element.200) | data formatting | bytes 4194304 | tf_op jit(solution)/shard_map/slice | solution.py:62
  340.4 35.9 %while.26 = (s32[]{:T(128)}, bf16[4,64,8,128]{3,1,2,0:T(8,128)(2,1)}, bf16[4,2048,128]{1,2,0:T(8,128)(2,1)}, bf16[4,2048,128]{1,2,0:T(8,128)(2,1)}, bf16[4,64,8,...) while((s32[]{:T(128)}, bf16[4,64,8,128]{3,1,2,0:T(8,128)(2,1)}, ...), condition=%wide.region_11.12_spmd.clone, body=%wide.region_8.11_spmd.clone.sunk | while | flops 813697024 | bytes 11410001 | solution.py:74
  340.6 5.0 %fusion.133 = (f32[8,64]{1,0:T(8,128)S(1)}, f32[8,64,2048]{2,1,0:T(8,128)}) fusion(pred[64,2048]{1,0:T(8,128)(4,1)S(1)} %bitcast.243, bf16[4,2048,128]{1,2,0:T(8,128)(2,1)} %get-tuple-element.304, s32[]{:T(128)} %get-tuple-element.294, bf16[1,64,8,128]{3,2,0,1:T(8,128)(2,1)S(1)} %constant_dynamic-slice_fusion.4), kind=kOutput, calls=%fused_computation.132.clone.1 | convolution fusion | flops 543164416 | bytes 5770240 | tf_op jit(solution)/shard_map/while/body/eval_jaxpr/sub | solution.py:70
  345.6 3.8 fusion.134
  349.6 5.1 %fusion.133 = (f32[8,64]{1,0:T(8,128)S(1)}, f32[8,64,2048]{2,1,0:T(8,128)}) fusion(pred[64,2048]{1,0:T(8,128)(4,1)S(1)} %bitcast.243, bf16[4,2048,128]{1,2,0:T(8,128)(2,1)} %get-tuple-element.304, s32[]{:T(128)} %get-tuple-element.294, bf16[1,64,8,128]{3,2,0,1:T(8,128)(2,1)S(1)} %constant_dynamic-slice_fusion.4), kind=kOutput, calls=%fused_computation.132.clone.1 | convolution fusion | flops 543164416 | bytes 5770240 | tf_op jit(solution)/shard_map/while/body/eval_jaxpr/sub | solution.py:70
  354.6 3.8 fusion.134
  358.6 4.9 %fusion.133 = (f32[8,64]{1,0:T(8,128)S(1)}, f32[8,64,2048]{2,1,0:T(8,128)}) fusion(pred[64,2048]{1,0:T(8,128)(4,1)S(1)} %bitcast.243, bf16[4,2048,128]{1,2,0:T(8,128)(2,1)} %get-tuple-element.304, s32[]{:T(128)} %get-tuple-element.294, bf16[1,64,8,128]{3,2,0,1:T(8,128)(2,1)S(1)} %constant_dynamic-slice_fusion.4), kind=kOutput, calls=%fused_computation.132.clone.1 | convolution fusion | flops 543164416 | bytes 5770240 | tf_op jit(solution)/shard_map/while/body/eval_jaxpr/sub | solution.py:70
  363.6 3.8 fusion.134
  367.6 4.9 %fusion.133 = (f32[8,64]{1,0:T(8,128)S(1)}, f32[8,64,2048]{2,1,0:T(8,128)}) fusion(pred[64,2048]{1,0:T(8,128)(4,1)S(1)} %bitcast.243, bf16[4,2048,128]{1,2,0:T(8,128)(2,1)} %get-tuple-element.304, s32[]{:T(128)} %get-tuple-element.294, bf16[1,64,8,128]{3,2,0,1:T(8,128)(2,1)S(1)} %constant_dynamic-slice_fusion.4), kind=kOutput, calls=%fused_computation.132.clone.1 | convolution fusion | flops 543164416 | bytes 5770240 | tf_op jit(solution)/shard_map/while/body/eval_jaxpr/sub | solution.py:70
  372.5 3.8 fusion.134
  (89 shorter events, 28.9 us)
Async XLA Ops:
  7.2 113.6 %copy-start = (bf16[1280,1280]{1,0:T(8,128)(2,1)S(1)}, bf16[1280,1280]{1,0:T(8,128)(2,1)}, u32[]{:S(2)}) copy-start(bf16[1280,1280]{1,0:T(8,128)(2,1)} %param.19) | copy-start | bytes 9830404
  7.2 93.9 %all-gather.5.cloned.1.call-start = ((), (), s32[]{:S(2)}) async-start(), calls=%async_computation.1 | async-start | bytes 10137600 | tf_op jit(solution)/shard_map/all_gather | solution.py:97
  7.9 198.2 %all-gather.7.cloned.1.call-start = ((), (), s32[]{:S(2)}) async-start(), calls=%async_computation.2 | async-start | bytes 4718592 | tf_op jit(solution)/shard_map/all_gather | solution.py:132
  125.7 3.2 copy-start.2
  126.8 28.9 %copy-start.5 = (s32[8,16]{1,0:T(8,128)S(1)}, s32[8,16]{1,0:T(8,128)}, u32[]{:S(2)}) copy-start(s32[8,16]{1,0:T(8,128)} %param.27) | copy-start | bytes 1540
  126.9 29.3 %copy-start.6 = (s32[8,2]{0,1:T(2,128)S(1)}, s32[8,2]{0,1:T(2,128)}, u32[]{:S(2)}) copy-start(s32[8,2]{0,1:T(2,128)} %param.28) | copy-start | bytes 196
  129.0 80.7 %copy-start.7 = (s32[8]{0:T(128)S(1)}, s32[8]{0:T(128)}, u32[]{:S(2)}) copy-start(s32[8]{0:T(128)} %param.29) | copy-start | bytes 100
  129.0 81.3 %copy-start.3 = (bf16[64,4096]{1,0:T(8,128)(2,1)S(1)}, bf16[64,4096]{1,0:T(8,128)(2,1)}, u32[]{:S(2)}) copy-start(bf16[64,4096]{1,0:T(8,128)(2,1)} %param.24) | copy-start | bytes 1572868
  129.1 81.3 %copy-start.4 = (bf16[64,4096]{1,0:T(8,128)(2,1)S(1)}, bf16[64,4096]{1,0:T(8,128)(2,1)}, u32[]{:S(2)}) copy-start(bf16[64,4096]{1,0:T(8,128)(2,1)} %param.25) | copy-start | bytes 1572868
  154.8 113.5 %all-gather.11.cloned.1.call-start = ((), (), s32[]{:S(2)}) async-start(), calls=%async_computation.4 | async-start | bytes 4325376 | tf_op jit(solution)/shard_map/all_gather | solution.py:143
  155.5 173.7 %all-gather.9.cloned.1.call-start = ((), (), s32[]{:S(2)}) async-start(), calls=%async_computation.3 | async-start | bytes 4325376 | tf_op jit(solution)/shard_map/all_gather | solution.py:140
  376.3 2.5 copy-start.1
Sparse Core Ops, SparseCore 0:
  10.6 90.3 all-gather.4
  154.9 51.1 all-gather.6
  208.6 59.5 all-gather.10
  271.3 57.8 all-gather.8
where the time goes:
time: 386 us; the launch traced here: 385 us
  waiting for transfers between devices  213 us (55%)
  matrix products  87.9 us (23%)
  local copies, waits for them, and re-layouts  35.8 us (9%)
  blocking collectives  24.6 us (6%)
  between operations  14 us (4%)
  other arithmetic  9.52 us (2%)
    all_gather x1, waiting for transfers between devices, per_device(): lax.all_gather(w_qkv, 'dev', axis=0, tiled=True)  89.5 us
    all_gather x1, waiting for transfers between devices, per_device(): text_all = lax.all_gather(text_kv, 'dev', axis=0, tiled=True)  57 us
    all_gather x1, waiting for transfers between devices, per_device(): gathered = lax.all_gather(blocks, 'group', axis=0, tiled=True)  49.1 us
    sub x8, matrix products, one_head(): exponent = jnp.where(key_mask, jnp.exp(scores - highest), 0.0)  39.8 us
    dot_general x8, matrix products, one_head(): jnp.einsum('grk,kd->rgd', weights, value_head, preferred_element_type=jnp...  27.7 us
    all_to_all x1, blocking collectives, per_device(): lax.all_to_all(kv_rows.reshape(tiles_dev, dev_count, row_block, channels)...  24.6 us
    all_gather x1, waiting for transfers between devices, per_device(): lax.all_gather(picked, 'dev', axis=1, tiled=True)  16 us
    slice x3, local copies, waits for them, and re-layouts, attend(): keyvals[:, :KVH * HD].reshape(key_count, KVH, HD).transpose(1, 0, 2)  10.1 us
  transfers between devices with their start and end apart: 4, of which 4 were waited for; matrix products, arithmetic and copies ran while one was open for 14% of the time, Pallas kernels for 0%

commit v1 on v0

v1 whole, which is shorter than its diff:
```python
import math

import jax
import jax.numpy as jnp
from jax import lax
from jax.experimental import pallas as pl
from jax.experimental.pallas import tpu as pltpu
from jax.sharding import PartitionSpec as P

RING = 4
VHD = 80
HD = 128
KVH = 4
GQ = 8
SLOTS = 2
IMG_G = 16
TILE_ROWS = 256
DV = 1280
PART = 480
HALF = 160
SLOT_SPAN = 1024
LOG2E = math.log2(math.e)
LOW = -1e30
BF = jnp.bfloat16
F32 = jnp.float32
VM = pl.BlockSpec(memory_space=pltpu.VMEM)
SM = pl.BlockSpec(memory_space=pltpu.SMEM)


def shape(rows, cols):
    return jax.ShapeDtypeStruct((rows, cols), BF)


def call(body, outs, scalars, arrays, scratch=(), limit=40, flops=0):
    return pl.pallas_call(
        body,
        out_shape=outs,
        in_specs=[SM] * len(scalars) + [VM] * len(arrays),
        out_specs=[VM] * len(outs),
        scratch_shapes=list(scratch),
        compiler_params=pltpu.CompilerParams(vmem_limit_bytes=limit << 20),
        cost_estimate=pl.CostEstimate(flops=flops, bytes_accessed=1 << 20, transcendentals=0),
    )(*scalars, *arrays)


def x_shift(value, k):
    return lax.ppermute(value, "dev", [(i, (i // 8) * 8 + (i + 2 * k) % 8) for i in range(32)])


def z_shift(value, k):
    return lax.ppermute(value, "dev", [(i, (i + 8 * k) % 32) for i in range(32)])


def core_swap(value):
    return lax.ppermute(value, "dev", [(i, i ^ 1) for i in range(32)])


def aligned(value, unit):
    return pl.multiple_of(value * unit, unit)


def split_tile_body(pos, tile, *outs):
    for k in range(RING):
        outs[k][...] = tile[pl.ds(aligned((pos[1] + k) % RING, 64), 64), :]


def pack_body(pos, *refs):
    ins, outs = refs[:RING], refs[RING:]
    for k in range(RING):
        for j in range(RING):
            outs[k][16 * j : 16 * j + 16, :] = ins[j][pl.ds(aligned((pos[0] + k) % RING, 16), 16), :]


def first_of(tpi, image):
    row, col = image // IMG_G, image % IMG_G
    total = jnp.int32(0)
    for j in range(IMG_G):
        total = total + jnp.where(j < col, tpi[row * IMG_G + j], 0)
    return total


def select_body(pos, tpi, table, *refs):
    ins, out, held = refs[:RING], refs[RING], refs[RING + 1]
    for k in range(RING):
        held[64 * k : 64 * k + 64, :] = ins[k][...]
    for item in range(8 * SLOTS):
        first = first_of(tpi, table[item])
        for u in range(2):
            step = ((pos[2] + first) & 1) + 2 * u
            chip = jnp.minimum(first + step, 31) // 2
            zk = (pos[0] - chip // RING + RING) % RING
            xk = (pos[1] - chip % RING + RING) % RING
            row = (item * 2 + u) * 16
            out[row : row + 16, :] = held[pl.ds(aligned(zk * RING + xk, 16), 16), :]


def pick_body(pos, table, *refs):
    for k in range(RING):
        refs[RING + k][...] = refs[k][...]


def pick(pos, table, received):
    def at(k):
        def index(i, pos, table):
            entry = (pos[0] + k) % RING
            return ((table[pos[3] * SLOTS + entry // 2] // IMG_G) * RING + entry, 0)

        return pl.BlockSpec((16, DV), index)

    return pl.pallas_call(
        pick_body,
        out_shape=[shape(16, DV)] * RING,
        grid_spec=pltpu.PrefetchScalarGridSpec(
            num_scalar_prefetch=2,
            grid=(1,),
            in_specs=[at(k) for k in range(RING)],
            out_specs=[pl.BlockSpec((16, DV), lambda i, pos, table: (0, 0))] * RING,
        ),
    )(pos, table, *([received] * RING))


def split_w_body(pos, w, mine, theirs):
    first = pos[2] == 0
    for p in range(RING):
        for j in range(3):
            at = j * DV + p * 2 * HALF
            lo, hi = w[:, at : at + HALF], w[:, at + HALF : at + 2 * HALF]
            mine[p, :, j * HALF : (j + 1) * HALF] = jnp.where(first, lo, hi)
            theirs[p, :, j * HALF : (j + 1) * HALF] = jnp.where(first, hi, lo)


def split_cols_body(pos, kv, cq, *outs):
    for k in range(RING):
        head = (pos[1] + k) % RING
        outs[k][:, :HD] = kv[:, pl.ds(aligned(head, HD), HD)]
        outs[k][:, HD:] = kv[:, pl.ds(aligned(head + KVH, HD), HD)]
        outs[RING + k][...] = cq[:, pl.ds(aligned(head, GQ * HD), GQ * HD)]


def assemble_rows(pos, blocks, tile):
    for k in range(RING):
        tile[pl.ds(aligned((pos[1] - k + RING) % RING, 64), 64), :] = blocks[k][...]


def encode_body(pos, gain, bias, *refs):
    blocks, weights = refs[:RING], refs[RING : 3 * RING]
    out, tile, held = refs[3 * RING], refs[3 * RING + 1], refs[3 * RING + 2 :]
    assemble_rows(pos, blocks, tile)
    for half in range(2):
        for zk in range(RING):
            for xk in range(RING):
                row = ((pos[0] - zk + RING) % RING) * RING + (pos[1] - xk + RING) % RING
                held[half][pl.ds(aligned(row, 80), 80), :] = weights[half * RING + zk][80 * xk : 80 * xk + 80, :]
    value = tile[...].astype(F32)
    center = jnp.mean(value, axis=-1, keepdims=True)
    value = value - center
    spread = jnp.mean(jnp.square(value), axis=-1, keepdims=True)
    normed = (value * lax.rsqrt(spread + 1e-05) * gain[...] + bias[...]).astype(BF)
    lane = lax.broadcasted_iota(jnp.int32, (TILE_ROWS, HALF), 1)
    scale = LOG2E / math.sqrt(VHD)
    for half in range(2):
        qkv = jnp.dot(normed, held[half][...], preferred_element_type=F32).astype(BF)
        query, key, value = qkv[:, :HALF], qkv[:, HALF : 2 * HALF], qkv[:, 2 * HALF :]
        context = jnp.zeros((TILE_ROWS, HALF), F32)
        for h in range(2):
            mine = (lane < VHD) == (h == 0)
            zero = jnp.zeros((), BF)
            scores = lax.dot_general(
                jnp.where(mine, query, zero), key, (((1,), (1,)), ((), ())), preferred_element_type=F32
            )
            highest = jnp.max(scores, axis=-1, keepdims=True)
            exponent = jnp.exp2((scores - highest) * scale)
            total = jnp.sum(exponent, axis=-1, keepdims=True)
            weight = (exponent / total).astype(BF)
            context = context + jnp.dot(weight, jnp.where(mine, value, zero), preferred_element_type=F32)
        out[:, half * HALF : (half + 1) * HALF] = context.astype(BF)


def project_body(pos, k_gain, w_out, w_kv, *refs):
    blocks, contexts = refs[:RING], refs[RING : 2 * RING]
    out, tile, held = refs[2 * RING :]
    assemble_rows(pos, blocks, tile)
    total = tile[...].astype(F32)
    for k in range(RING):
        part = (pos[1] - k + RING) % RING
        held[:HALF, :] = w_out[pl.ds(aligned(part * 2 + pos[2], HALF), HALF), :]
        held[HALF:, :] = w_out[pl.ds(aligned(part * 2 + 1 - pos[2], HALF), HALF), :]
        total = total + jnp.dot(contexts[k][...], held[...], preferred_element_type=F32)
    residual = total.astype(BF)
    key = jnp.dot(residual, w_kv[:, pl.ds(aligned(pos[1], HD), HD)], preferred_element_type=F32)
    value = jnp.dot(residual, w_kv[:, pl.ds(aligned(pos[1] + KVH, HD), HD)], preferred_element_type=F32)
    key = key * lax.rsqrt(jnp.mean(jnp.square(key), axis=-1, keepdims=True) + 1e-06) * k_gain[...]
    out[:, :HD] = key.astype(BF)
    out[:, HD:] = value.astype(BF)


BLOCK = 256


def softmax_rows(query, keys, values, seen):
    scores = lax.dot_general(query, keys, (((1,), (1,)), ((), ())), preferred_element_type=F32)
    scores = seen(scores)
    highest = jnp.max(scores, axis=-1, keepdims=True)
    exponent = jnp.exp2((scores - highest) * (LOG2E / math.sqrt(HD)))
    total = jnp.sum(exponent, axis=-1, keepdims=True)
    result = jnp.dot(exponent.astype(BF), values, preferred_element_type=F32)
    return (result / total).astype(BF)


def cross_body(pos, tpi, table, offsets, *refs):
    queries, pieces = refs[:RING], refs[RING : 3 * RING]
    outs = refs[3 * RING : 4 * RING]
    held_q, held_o, held_k, held_v = refs[4 * RING :]
    for k in range(RING):
        for h in range(GQ):
            held_q[(k * GQ + h) * 64 : (k * GQ + h + 1) * 64, :] = queries[k][:, h * HD : (h + 1) * HD]
    for n in range(2 * RING):
        held_k[n * TILE_ROWS : (n + 1) * TILE_ROWS, :] = pieces[n][:, :HD]
        held_v[n * TILE_ROWS : (n + 1) * TILE_ROWS, :] = pieces[n][:, HD:]
    group = pos[3]
    slot_of, low_of = [], []
    images = [table[group * SLOTS + s] for s in range(SLOTS)]
    firsts = [first_of(tpi, image) for image in images]
    counts = [tpi[image] for image in images]
    for n in range(2 * RING):
        entry = (pos[0] - n % RING + RING) % RING
        slot, u = entry // 2, entry % 2
        core = pos[2] if n < RING else 1 - pos[2]
        first = jnp.where(slot == 0, firsts[0], firsts[1])
        count = jnp.where(slot == 0, counts[0], counts[1])
        step = ((core + first) & 1) + 2 * u
        slot_of.append(slot)
        low_of.append(jnp.where(step < count, 0.0, LOW).astype(F32))

    def block(i, carry):
        at = pl.ds(pl.multiple_of(i * BLOCK, BLOCK), BLOCK)
        source = (pos[1] - i // (GQ * 64 // BLOCK) + RING) % RING
        start = offsets[group] + pos[0] * 512 + source * 128 + pos[2] * 64
        row = lax.broadcasted_iota(jnp.int32, (BLOCK, 1), 0)
        position = start + row % 64

        def seen(scores):
            parts = []
            for n in range(2 * RING):
                low = jnp.where(position >= slot_of[n] * SLOT_SPAN, low_of[n], LOW)
                parts.append(scores[:, n * TILE_ROWS : (n + 1) * TILE_ROWS] + low)
            return jnp.concatenate(parts, axis=1)

        held_o[at, :] = softmax_rows(held_q[at, :], held_k[...], held_v[...], seen)
        return carry

    lax.fori_loop(0, RING * GQ * 64 // BLOCK, block, 0)
    for k in range(RING):
        for h in range(GQ):
            outs[k][:, h * HD : (h + 1) * HD] = held_o[(k * GQ + h) * 64 : (k * GQ + h + 1) * 64, :]


def self_body(pos, queries, kv, out, held_q, held_o):
    span = kv.shape[0]
    rows = queries.shape[0]
    for h in range(KVH * GQ):
        held_q[h * rows : (h + 1) * rows, :] = queries[:, h * HD : (h + 1) * HD]
    start = ((pos[0] * RING + pos[1]) * 2 + pos[2]) * rows

    def block(i, carry):
        at = pl.ds(pl.multiple_of(i * BLOCK, BLOCK), BLOCK)
        head = i // (GQ * rows // BLOCK)
        keys = kv[:, pl.ds(aligned(head, HD), HD)]
        values = kv[:, pl.ds(aligned(head + KVH, HD), HD)]
        row = start + lax.broadcasted_iota(jnp.int32, (BLOCK, 1), 0) % rows
        col = lax.broadcasted_iota(jnp.int32, (1, span), 1)
        held_o[at, :] = softmax_rows(
            held_q[at, :], keys, values, lambda scores: jnp.where(col <= row, scores, LOW)
        )
        return carry

    lax.fori_loop(0, KVH * GQ * rows // BLOCK, block, 0)
    for h in range(KVH * GQ):
        out[:, h * HD : (h + 1) * HD] = held_o[h * rows : (h + 1) * rows, :]


def place_body(pos, *refs):
    ins, out = refs[:RING], refs[RING]
    for k in range(RING):
        out[:, pl.ds(aligned((pos[1] + k) % RING, GQ * HD), GQ * HD)] = ins[k][...]


def per_device(
    tiles,
    w_qkv,
    w_out,
    w_kv,
    ln_gain,
    ln_bias,
    k_gain,
    cross_queries,
    self_queries,
    text_kv,
    tiles_per_image,
    request_table,
    span_offsets,
):
    dev = lax.axis_index("dev")
    pos = jnp.stack([dev // 8, (dev // 2) % 4, dev % 2, lax.axis_index("group")]).astype(jnp.int32)
    tpi = tiles_per_image.reshape(-1)
    table = request_table.reshape(-1)
    span_kv = lax.all_gather(text_kv, "dev", axis=0, tiled=True)

    blocks = call(split_tile_body, [shape(64, DV)] * RING, (pos,), (tiles.reshape(TILE_ROWS, DV),))
    spread = [blocks[0]] + [x_shift(blocks[k], k) for k in (1, 2, 3)]

    mine, theirs = pl.pallas_call(
        split_w_body,
        out_shape=[jax.ShapeDtypeStruct((RING, 40, PART), BF)] * 2,
        in_specs=[SM, VM],
        out_specs=[VM] * 2,
    )(pos, w_qkv)
    got = core_swap(theirs)
    even = pos[2] == 0
    pair = jnp.concatenate([jnp.where(even, mine, got), jnp.where(even, got, mine)], axis=1)
    parts = [lax.dynamic_index_in_dim(pair, (pos[1] + k) % RING, 0, keepdims=False) for k in range(RING)]
    parts = jnp.concatenate([parts[0]] + [x_shift(parts[k], k) for k in (1, 2, 3)], axis=0)

    cols = call(
        split_cols_body,
        [shape(64, 2 * HD)] * RING + [shape(64, GQ * HD)] * RING,
        (pos,),
        (text_kv, cross_queries),
    )
    cq = [cols[RING]] + [x_shift(cols[RING + k], k) for k in (1, 2, 3)]

    packed = call(pack_body, [shape(64, DV)] * RING, (pos,), tuple(spread))
    packed = [packed[0]] + [z_shift(packed[k], k) for k in (1, 2, 3)]
    weights = [parts] + [z_shift(parts, k) for k in (1, 2, 3)]

    chosen = call(
        select_body,
        [shape(8 * 64, DV)],
        (pos, tpi, table),
        tuple(packed),
        [pltpu.VMEM((TILE_ROWS, DV), BF)],
    )[0]
    received = lax.all_to_all(chosen.reshape(8, 64, DV), "group", 0, 0, tiled=True).reshape(8 * 64, DV)
    picked = pick(pos, table, received)
    rows = jnp.concatenate([picked[0]] + [z_shift(picked[k], k) for k in (1, 2, 3)], axis=0)
    blocks = [rows] + [x_shift(rows, k) for k in (1, 2, 3)]

    weights = weights + [core_swap(value) for value in weights]
    context = call(
        encode_body,
        [shape(TILE_ROWS, 2 * HALF)],
        (pos,),
        (ln_gain.reshape(1, DV), ln_bias.reshape(1, DV), *blocks, *weights),
        [pltpu.VMEM((TILE_ROWS, DV), BF), pltpu.VMEM((DV, PART), BF), pltpu.VMEM((DV, PART), BF)],
        flops=1 << 30,
    )[0]
    contexts = [context] + [x_shift(context, k) for k in (1, 2, 3)]
    piece = call(
        project_body,
        [shape(TILE_ROWS, 2 * HD)],
        (pos,),
        (k_gain.reshape(1, HD), w_out, w_kv, *blocks, *contexts),
        [pltpu.VMEM((TILE_ROWS, DV), BF), pltpu.VMEM((2 * HALF, DV), BF)],
        flops=1 << 30,
    )[0]
    pieces = [piece] + [z_shift(piece, k) for k in (1, 2, 3)]
    pieces = pieces + [core_swap(value) for value in pieces]
    stack = RING * GQ * 64
    tokens = cross_queries.shape[0]
    back = call(
        cross_body,
        [shape(64, GQ * HD)] * RING,
        (pos, tpi, table, span_offsets),
        (*cq, *pieces),
        [pltpu.VMEM((stack, HD), BF)] * 4,
        flops=1 << 32,
    )
    back = [back[0]] + [x_shift(back[k], RING - k) for k in (1, 2, 3)]
    cross_out = call(place_body, [shape(tokens, RING * GQ * HD)], (pos,), tuple(back))[0]
    self_out = call(
        self_body,
        [shape(tokens, KVH * GQ * HD)],
        (pos,),
        (self_queries, span_kv),
        [pltpu.VMEM((stack, HD), BF)] * 2,
        flops=1 << 32,
    )[0]
    return (cross_out, self_out)


def solution(mesh):
    in_specs = (
        P(("group", "dev"), None, None),
        P("dev", None),
        P(),
        P(),
        P(),
        P(),
        P(),
        P(("group", "dev"), None),
        P(("group", "dev"), None),
        P(("group", "dev"), None),
        P(),
        P(),
        P(),
    )
    out_specs = (P(("group", "dev"), None), P(("group", "dev"), None))
    return jax.shard_map(
        per_device, mesh=mesh, in_specs=in_specs, out_specs=out_specs, check_vma=False
    )
```

time: 386 us -> 232 us (0.60)
  waiting for transfers between devices: 213 us -> 75.3 us
  starting transfers between devices: 0.34 us -> 93.2 us
  matrix products: 87.9 us -> 0 us
  Pallas kernels: 0 us -> 40.5 us
  local copies, waits for them, and re-layouts: 35.8 us -> 6.85 us
  blocking collectives: 24.6 us -> 0 us
  other arithmetic: 9.52 us -> 1.1 us
    all_gather x4 -> x1, waiting for transfers between devices: 212 us -> 0.01 us  [per_device(): span_kv = lax.all_gather(text_kv, 'dev', axis=0, tiled=True)]
    ppermute x0 -> x39, starting transfers between devices: none -> 89.6 us  [the longest x12 33.4 us: z_shift(): lax.ppermute(value, 'dev', [(i, (i + 8 * k) % 32) for i in range(32)])]
    ppermute x0 -> x39, waiting for transfers between devices: none -> 74.6 us  [the longest x12 46.7 us: z_shift(): lax.ppermute(value, 'dev', [(i, (i + 8 * k) % 32) for i in range(32)])]
    dot_general x13 -> x0, matrix products: 48.1 us -> none  [the longest x8 27.7 us: one_head(): jnp.einsum('grk,kd->rgd', weights, value_head, preferred_element_type=jnp...]
    pallas_call x0 -> x11, Pallas kernels: none -> 40.5 us  [the longest x9 35.8 us: call(): pl.pallas_call(body, out_shape=outs, in_specs=[SM] * len(scalars) + [VM]...]
    sub x8 -> x0, matrix products: 39.8 us -> none  [one_head(): exponent = jnp.where(key_mask, jnp.exp(scores - highest), 0.0)]
    all_to_all x1 -> x0, blocking collectives: 24.6 us -> none  [per_device(): lax.all_to_all(kv_rows.reshape(tiles_dev, dev_count, row_block, channels)...]
    slice x4 -> x0, local copies, waits for them, and re-layouts: 14.1 us -> none  [the longest x3 10.1 us: attend(): keyvals[:, :KVH * HD].reshape(key_count, KVH, HD).transpose(1, 0, 2)]
  transfers between devices with their start and end apart: 4 -> 41, of which waited for: 4 -> 21; matrix products, arithmetic and copies ran while one was open for 14% -> 2% of each run, Pallas kernels for 0% -> 12%
where the time goes in v1:
time: 232 us; the launch traced here: 231 us
  starting transfers between devices  93.2 us (40%)
  waiting for transfers between devices  75.3 us (32%)
  Pallas kernels  40.5 us (17%)
  between operations  14.3 us (6%)
  local copies, waits for them, and re-layouts  6.85 us (3%)
    ppermute x12, waiting for transfers between devices, z_shift(): lax.ppermute(value, 'dev', [(i, (i + 8 * k) % 32) for i in range(32)])  46.7 us
    pallas_call x9, Pallas kernels, call(): pl.pallas_call(body, out_shape=outs, in_specs=[SM] * len(scalars) + [VM]...  35.8 us
    ppermute x12, starting transfers between devices, z_shift(): lax.ppermute(value, 'dev', [(i, (i + 8 * k) % 32) for i in range(32)])  33.4 us
    ppermute x9, starting transfers between devices, core_swap(): return lax.ppermute(value, 'dev', [(i, i ^ 1) for i in range(32)])  30.1 us
    ppermute x18, starting transfers between devices, x_shift(): lax.ppermute(value, 'dev', [(i, i // 8 * 8 + (i + 2 * k) % 8) for i in ra...  26.1 us
    ppermute x18, waiting for transfers between devices, x_shift(): lax.ppermute(value, 'dev', [(i, i // 8 * 8 + (i + 2 * k) % 8) for i in ra...  25.3 us
    unnamed x36, local copies, waits for them, and re-layouts  5.99 us
  transfers between devices with their start and end apart: 41, of which 21 were waited for; matrix products, arithmetic and copies ran while one was open for 2% of the time, Pallas kernels for 12%

profile of v1, /device:TPU:1, one launch (start us, length us, event | category | flops | bytes accessed | tf_op | source)
XLA Modules:
  0.0 231.2 jit_solution(6905782853183855270)
XLA Ops:
  11.8 2.5 %collective-permute-start.4 = (bf16[64,1280]{1,0:T(8,128)(2,1)S(1)}, bf16[64,1280]{1,0:T(8,128)(2,1)S(1)}, u32[]{:S(2)}, u32[]{:S(2)}) collective-permute-start(bf16[64,1280]{1,0:T(8,128)(2,1)S(1)} %get-tuple-element.30), channel_id=1, source_target_pairs={{0,4},{1,5},{2,6},{3,7},{4,0},{5,1},{6,2},{7,3},{8,12},{9,13},{10,... | collective-permute-start | bytes 491528 | tf_op jit(solution)/shard_map/ppermute | solution.py:47
  15.8 5.6 %collective-permute-done.4.refs_2_ = bf16[64,1280]{1,0:T(8,128)(2,1)S(1)} collective-permute-done((bf16[64,1280]{1,0:T(8,128)(2,1)S(1)}, bf16[64,1280]{1,0:T(8,128)(2,1)S(1)}, u32[]{:S(2)}, u32[]{:S(2)}) %collective-permute-start.4) | collective-permute-done | bytes 163872 | tf_op jit(solution)/shard_map/ppermute | solution.py:47
  22.0 3.0 %collective-permute-start.6 = (bf16[64,1280]{1,0:T(8,128)(2,1)S(1)}, bf16[64,1280]{1,0:T(8,128)(2,1)S(1)}, u32[]{:S(2)}, u32[]{:S(2)}) collective-permute-start(bf16[64,1280]{1,0:T(8,128)(2,1)S(1)} %get-tuple-element.33), channel_id=1, source_target_pairs={{0,8},{1,9},{2,10},{3,11},{4,12},{5,13},{6,14},{7,15},{8,16},{9,17... | collective-permute-start | bytes 491528 | tf_op jit(solution)/shard_map/ppermute | solution.py:51
  25.1 5.1 %collective-permute-start.7 = (bf16[64,1280]{1,0:T(8,128)(2,1)S(1)}, bf16[64,1280]{1,0:T(8,128)(2,1)S(1)}, u32[]{:S(2)}, u32[]{:S(2)}) collective-permute-start(bf16[64,1280]{1,0:T(8,128)(2,1)S(1)} %get-tuple-element.34), channel_id=1, source_target_pairs={{0,16},{1,17},{2,18},{3,19},{4,20},{5,21},{6,22},{7,23},{8,24},{9,... | collective-permute-start | bytes 491528 | tf_op jit(solution)/shard_map/ppermute | solution.py:51
  30.2 2.4 %collective-permute-start.8 = (bf16[64,1280]{1,0:T(8,128)(2,1)S(1)}, bf16[64,1280]{1,0:T(8,128)(2,1)S(1)}, u32[]{:S(2)}, u32[]{:S(2)}) collective-permute-start(bf16[64,1280]{1,0:T(8,128)(2,1)S(1)} %get-tuple-element.35), channel_id=1, source_target_pairs={{0,24},{1,25},{2,26},{3,27},{4,28},{5,29},{6,30},{7,31},{8,0},{9,1... | collective-permute-start | bytes 491528 | tf_op jit(solution)/shard_map/ppermute | solution.py:51
  34.2 6.2 %collective-permute-done.7.refs_2_ = bf16[64,1280]{1,0:T(8,128)(2,1)S(1)} collective-permute-done((bf16[64,1280]{1,0:T(8,128)(2,1)S(1)}, bf16[64,1280]{1,0:T(8,128)(2,1)S(1)}, u32[]{:S(2)}, u32[]{:S(2)}) %collective-permute-start.7) | collective-permute-done | bytes 163872 | tf_op jit(solution)/shard_map/ppermute | solution.py:51
  40.4 8.1 %collective-permute-done.8.refs_3_ = bf16[64,1280]{1,0:T(8,128)(2,1)S(1)} collective-permute-done((bf16[64,1280]{1,0:T(8,128)(2,1)S(1)}, bf16[64,1280]{1,0:T(8,128)(2,1)S(1)}, u32[]{:S(2)}, u32[]{:S(2)}) %collective-permute-start.8) | collective-permute-done | bytes 163872 | tf_op jit(solution)/shard_map/ppermute | solution.py:51
  48.5 2.7 %shard_map.143 = bf16[512,1280]{1,0:T(8,128)(2,1)} custom-call(s32[4]{0:T(128)S(1)} %pad_add_fusion.pos, s32[128]{0:T(128)S(1)} %reshape.28.tpi, s32[16]{0:T(128)S(1)} %reshape.29.table, bf16[64,1280]{1,0:T(8,128)(2,1)S(1)} %get-tuple-element.32.refs_0_, bf16[64,1280]{1,0:T(8,128)(2,1)S(1)} %collective-permute-done.6.refs_1_, ...), custom_call_target="tpu_custom_call" | custom-call | bytes 1048576 | tf_op jit(solution)/shard_map/pallas_call | solution.py:35
  51.3 3.6 %all-to-all-start = ((bf16[8,64,1280]{2,1,0:T(8,128)(2,1)}), bf16[8,64,1280]{2,1,0:T(8,128)(2,1)S(1)}, u32[]{:S(2)}, u32[]{:S(2)}) async-start(bf16[8,64,1280]{2,1,0:T(8,128)(2,1)} %bitcast.6), calls=%async_computation | async-start | bytes 2621440 | tf_op jit(solution)/shard_map/all_to_all | solution.py:343
  54.8 2.4 %shard_map.145 = (bf16[4,40,480]{2,1,0:T(8,128)(2,1)}, bf16[4,40,480]{2,1,0:T(8,128)(2,1)}) custom-call(s32[4]{0:T(128)} %copy-done.5, bf16[40,3840]{1,0:T(8,128)(2,1)} %w.1), custom_call_target="tpu_custom_call" | custom-call | tf_op jit(solution)/shard_map/pallas_call | solution.py:312
  61.5 2.5 %collective-permute-start.18 = (bf16[80,480]{1,0:T(8,128)(2,1)S(1)}, bf16[80,480]{1,0:T(8,128)(2,1)S(1)}, u32[]{:S(2)}, u32[]{:S(2)}) collective-permute-start(bf16[80,480]{1,0:T(8,128)(2,1)S(1)} %get-tuple-element.49), channel_id=1, source_target_pairs={{0,6},{1,7},{2,0},{3,1},{4,2},{5,3},{6,4},{7,5},{8,14},{9,15},{10,... | collective-permute-start | bytes 230408 | tf_op jit(solution)/shard_map/ppermute | solution.py:47
  66.5 2.6 %collective-permute-done.17 = bf16[80,480]{1,0:T(8,128)(2,1)S(1)} collective-permute-done((bf16[80,480]{1,0:T(8,128)(2,1)S(1)}, bf16[80,480]{1,0:T(8,128)(2,1)S(1)}, u32[]{:S(2)}, u32[]{:S(2)}) %collective-permute-start.17) | collective-permute-done | bytes 76832 | tf_op jit(solution)/shard_map/ppermute | solution.py:47
  71.2 3.9 %collective-permute-start.19 = (bf16[320,480]{1,0:T(8,128)(2,1)S(1)}, bf16[320,480]{1,0:T(8,128)(2,1)S(1)}, u32[]{:S(2)}, u32[]{:S(2)}) collective-permute-start(bf16[320,480]{1,0:T(8,128)(2,1)S(1)} %pad_maximum_fusion.refs_4_), channel_id=1, source_target_pairs={{0,8},{1,9},{2,10},{3,11},{4,12},{5,13},{6,14},{7,15},{8,16},{9,17... | collective-permute-start | bytes 921608 | tf_op jit(solution)/shard_map/ppermute | solution.py:51
  75.9 2.8 %collective-permute-start.21 = (bf16[320,480]{1,0:T(8,128)(2,1)S(1)}, bf16[320,480]{1,0:T(8,128)(2,1)}, u32[]{:S(2)}, u32[]{:S(2)}) collective-permute-start(bf16[320,480]{1,0:T(8,128)(2,1)S(1)} %pad_maximum_fusion.refs_4_), channel_id=1, source_target_pairs={{0,24},{1,25},{2,26},{3,27},{4,28},{5,29},{6,30},{7,31},{8,0},{9,1... | collective-permute-start | bytes 921608 | tf_op jit(solution)/shard_map/ppermute | solution.py:51
  81.0 22.2 %collective-permute-done.19.refs_5_ = bf16[320,480]{1,0:T(8,128)(2,1)S(1)} collective-permute-done((bf16[320,480]{1,0:T(8,128)(2,1)S(1)}, bf16[320,480]{1,0:T(8,128)(2,1)S(1)}, u32[]{:S(2)}, u32[]{:S(2)}) %collective-permute-start.19) | collective-permute-done | bytes 307232 | tf_op jit(solution)/shard_map/ppermute | solution.py:51
  103.2 10.6 %collective-permute-start.23 = (bf16[320,480]{1,0:T(8,128)(2,1)S(1)}, bf16[320,480]{1,0:T(8,128)(2,1)}, u32[]{:S(2)}, u32[]{:S(2)}) collective-permute-start(bf16[320,480]{1,0:T(8,128)(2,1)S(1)} %collective-permute-done.19.refs_5_), channel_id=1, source_target_pairs={{0,1},{1,0},{2,3},{3,2},{4,5},{5,4},{6,7},{7,6},{8,9},{9,8},{10,11... | collective-permute-start | bytes 921608 | tf_op jit(solution)/shard_map/ppermute | solution.py:55
  115.5 2.3 %shard_map.144 = (bf16[16,1280]{1,0:T(8,128)(2,1)}, bf16[16,1280]{1,0:T(8,128)(2,1)}, bf16[16,1280]{1,0:T(8,128)(2,1)}, bf16[16,1280]{1,0:T(8,128)(2,1)}) custom-call(s32[4]{0:T(128)} %copy-done.5, s32[16]{0:T(128)} %copy-done.7, bf16[512,1280]{1,0:T(8,128)(2,1)} %bitcast.18, bf16[512,1280]{1,0:T(8,128)(2,1)} %bitcast.19, bf16[512,1280]{1,0:T(8,128)(2,1)} %bitcast.20, ...), custom_call_target="tpu_custom_call" | custom-call | tf_op jit(solution)/shard_map/pallas_call | solution.py:110
  117.8 7.2 %collective-permute-start.9 = (bf16[16,1280]{1,0:T(8,128)(2,1)}, bf16[16,1280]{1,0:T(8,128)(2,1)S(1)}, u32[]{:S(2)}, u32[]{:S(2)}) collective-permute-start(bf16[16,1280]{1,0:T(8,128)(2,1)} %get-tuple-element.37), channel_id=1, source_target_pairs={{0,8},{1,9},{2,10},{3,11},{4,12},{5,13},{6,14},{7,15},{8,16},{9,17... | collective-permute-start | bytes 122888 | tf_op jit(solution)/shard_map/ppermute | solution.py:51
  125.8 2.5 %collective-permute-done.9 = bf16[16,1280]{1,0:T(8,128)(2,1)S(1)} collective-permute-done((bf16[16,1280]{1,0:T(8,128)(2,1)}, bf16[16,1280]{1,0:T(8,128)(2,1)S(1)}, u32[]{:S(2)}, u32[]{:S(2)}) %collective-permute-start.9) | collective-permute-done | bytes 40992 | tf_op jit(solution)/shard_map/ppermute | solution.py:51
  129.9 5.4 %collective-permute-done.10 = bf16[16,1280]{1,0:T(8,128)(2,1)S(1)} collective-permute-done((bf16[16,1280]{1,0:T(8,128)(2,1)}, bf16[16,1280]{1,0:T(8,128)(2,1)S(1)}, u32[]{:S(2)}, u32[]{:S(2)}) %collective-permute-start.10) | collective-permute-done | bytes 40992 | tf_op jit(solution)/shard_map/ppermute | solution.py:51
  144.7 3.0 %collective-permute-done.13.refs_2_ = bf16[64,1280]{1,0:T(8,128)(2,1)S(1)} collective-permute-done((bf16[64,1280]{1,0:T(8,128)(2,1)S(1)}, bf16[64,1280]{1,0:T(8,128)(2,1)S(1)}, u32[]{:S(2)}, u32[]{:S(2)}) %collective-permute-start.13) | collective-permute-done | bytes 163872 | tf_op jit(solution)/shard_map/ppermute | solution.py:47
  147.7 4.4 %shard_map.146.refs_4_ = bf16[256,320]{1,0:T(8,128)(2,1)S(1)} custom-call(s32[4]{0:T(128)S(1)} %copy-done.6, f32[1,1280]{1,0:T(1,128)S(1)} %reshape.34.gain, f32[1,1280]{1,0:T(1,128)S(1)} %reshape.35.bias, bf16[64,1280]{1,0:T(8,128)(2,1)S(1)} %constant_dynamic-update-slice_fusion.refs_0_, bf16[64,1280]{1,0:T(8,128)(2,1)S(1)} %collective-permute-done.12.refs_1_, ...), custom_call_target="tpu_custom_call" | custom-call | flops 1073741824 | bytes 1048576 | tf_op jit(solution)/shard_map/pallas_call | solution.py:35
  161.0 2.8 %shard_map.147.refs_4_ = bf16[256,256]{1,0:T(8,128)(2,1)S(1)} custom-call(s32[4]{0:T(128)S(1)} %copy-done.6, f32[1,128]{1,0:T(1,128)S(1)} %bitcast.17, bf16[1280,1280]{1,0:T(8,128)(2,1)S(1)} %copy-done, bf16[1280,1024]{1,0:T(8,128)(2,1)S(1)} %copy-done.1, bf16[64,1280]{1,0:T(8,128)(2,1)S(1)} %constant_dynamic-update-slice_fusion.refs_0_, ...), custom_call_target="tpu_custom_call" | custom-call | flops 1073741824 | bytes 1048576 | tf_op jit(solution)/shard_map/pallas_call | solution.py:35
  165.2 3.2 %collective-permute-start.30 = (bf16[256,256]{1,0:T(8,128)(2,1)S(1)}, bf16[256,256]{1,0:T(8,128)(2,1)S(1)}, u32[]{:S(2)}, u32[]{:S(2)}) collective-permute-start(bf16[256,256]{1,0:T(8,128)(2,1)S(1)} %shard_map.147.refs_4_), channel_id=1, source_target_pairs={{0,16},{1,17},{2,18},{3,19},{4,20},{5,21},{6,22},{7,23},{8,24},{9,... | collective-permute-start | bytes 393224 | tf_op jit(solution)/shard_map/ppermute | solution.py:51
  168.6 2.4 %collective-permute-start.2 = (bf16[64,1024]{1,0:T(8,128)(2,1)S(1)}, bf16[64,1024]{1,0:T(8,128)(2,1)S(1)}, u32[]{:S(2)}, u32[]{:S(2)}) collective-permute-start(bf16[64,1024]{1,0:T(8,128)(2,1)S(1)} %get-tuple-element.27), channel_id=1, source_target_pairs={{0,6},{1,7},{2,0},{3,1},{4,2},{5,3},{6,4},{7,5},{8,14},{9,15},{10,... | collective-permute-start | bytes 393224 | tf_op jit(solution)/shard_map/ppermute | solution.py:47
  171.0 8.5 %collective-permute-start.32 = (bf16[256,256]{1,0:T(8,128)(2,1)S(1)}, bf16[256,256]{1,0:T(8,128)(2,1)S(1)}, u32[]{:S(2)}, u32[]{:S(2)}) collective-permute-start(bf16[256,256]{1,0:T(8,128)(2,1)S(1)} %shard_map.147.refs_4_), channel_id=1, source_target_pairs={{0,1},{1,0},{2,3},{3,2},{4,5},{5,4},{6,7},{7,6},{8,9},{9,8},{10,11... | collective-permute-start | bytes 393224 | tf_op jit(solution)/shard_map/ppermute | solution.py:55
  179.6 6.1 %collective-permute-start.34 = (bf16[256,256]{1,0:T(8,128)(2,1)S(1)}, bf16[256,256]{1,0:T(8,128)(2,1)S(1)}, u32[]{:S(2)}, u32[]{:S(2)}) collective-permute-start(bf16[256,256]{1,0:T(8,128)(2,1)S(1)} %collective-permute-done.30.refs_6_), channel_id=1, source_target_pairs={{0,1},{1,0},{2,3},{3,2},{4,5},{5,4},{6,7},{7,6},{8,9},{9,8},{10,11... | collective-permute-start | bytes 393224 | tf_op jit(solution)/shard_map/ppermute | solution.py:55
  187.1 10.2 %shard_map.148 = (bf16[64,1024]{1,0:T(8,128)(2,1)S(1)}, bf16[64,1024]{1,0:T(8,128)(2,1)S(1)}, bf16[64,1024]{1,0:T(8,128)(2,1)S(1)}, bf16[64,1024]{1,0:T(8,128)(2,1)S(1)}) custom-call(s32[4]{0:T(128)S(1)} %copy-done.6, s32[128]{0:T(128)S(1)} %reshape.28.tpi, s32[16]{0:T(128)S(1)} %copy-done.8, s32[8]{0:T(128)S(1)} %copy-done.12, ...), custom_call_target="tpu_custom_call" | custom-call | flops 4294967296 | bytes 1048576 | tf_op jit(solution)/shard_map/pallas_call | solution.py:35
  197.3 2.4 %collective-permute-start.36 = (bf16[64,1024]{1,0:T(8,128)(2,1)S(1)}, bf16[64,1024]{1,0:T(8,128)(2,1)S(1)}, u32[]{:S(2)}, u32[]{:S(2)}) collective-permute-start(bf16[64,1024]{1,0:T(8,128)(2,1)S(1)} %get-tuple-element.43), channel_id=1, source_target_pairs={{0,6},{1,7},{2,0},{3,1},{4,2},{5,3},{6,4},{7,5},{8,14},{9,15},{10,... | collective-permute-start | bytes 393224 | tf_op jit(solution)/shard_map/ppermute | solution.py:47
  203.1 2.4 %collective-permute-done.37.refs_2_ = bf16[64,1024]{1,0:T(8,128)(2,1)S(1)} collective-permute-done((bf16[64,1024]{1,0:T(8,128)(2,1)S(1)}, bf16[64,1024]{1,0:T(8,128)(2,1)S(1)}, u32[]{:S(2)}, u32[]{:S(2)}) %collective-permute-start.37) | collective-permute-done | bytes 131104 | tf_op jit(solution)/shard_map/ppermute | solution.py:47
  205.5 3.3 %collective-permute-done.38.refs_3_ = bf16[64,1024]{1,0:T(8,128)(2,1)S(1)} collective-permute-done((bf16[64,1024]{1,0:T(8,128)(2,1)S(1)}, bf16[64,1024]{1,0:T(8,128)(2,1)S(1)}, u32[]{:S(2)}, u32[]{:S(2)}) %collective-permute-start.38) | collective-permute-done | bytes 131104 | tf_op jit(solution)/shard_map/ppermute | solution.py:47
  212.5 11.9 %shard_map.150 = bf16[64,4096]{1,0:T(8,128)(2,1)} custom-call(s32[4]{0:T(128)S(1)} %copy-done.6, bf16[64,4096]{1,0:T(8,128)(2,1)S(1)} %copy-done.11, bf16[2048,1024]{1,0:T(8,128)(2,1)S(1)} %copy-done.10), custom_call_target="tpu_custom_call" | custom-call | flops 4294967296 | bytes 1048576 | tf_op jit(solution)/shard_map/pallas_call | solution.py:35
  (107 shorter events, 52.5 us)
Async XLA Ops:
  7.2 203.1 %all-gather.2.cloned.1.call-start = ((), (), s32[]{:S(2)}) async-start(), calls=%async_computation.1 | async-start | bytes 4325376 | tf_op jit(solution)/shard_map/all_gather | solution.py:307
  9.7 6.1 %collective-permute-start.3 = (bf16[64,1280]{1,0:T(8,128)(2,1)S(1)}, bf16[64,1280]{1,0:T(8,128)(2,1)S(1)}, u32[]{:S(2)}, u32[]{:S(2)}) collective-permute-start(bf16[64,1280]{1,0:T(8,128)(2,1)S(1)} %get-tuple-element.29), channel_id=1, source_target_pairs={{0,2},{1,3},{2,4},{3,5},{4,6},{5,7},{6,0},{7,1},{8,10},{9,11},{10,... | collective-permute-start | bytes 491528 | tf_op jit(solution)/shard_map/ppermute | solution.py:47
  11.8 9.6 %collective-permute-start.4 = (bf16[64,1280]{1,0:T(8,128)(2,1)S(1)}, bf16[64,1280]{1,0:T(8,128)(2,1)S(1)}, u32[]{:S(2)}, u32[]{:S(2)}) collective-permute-start(bf16[64,1280]{1,0:T(8,128)(2,1)S(1)} %get-tuple-element.30), channel_id=1, source_target_pairs={{0,4},{1,5},{2,6},{3,7},{4,0},{5,1},{6,2},{7,3},{8,12},{9,13},{10,... | collective-permute-start | bytes 491528 | tf_op jit(solution)/shard_map/ppermute | solution.py:47
  14.3 7.2 %collective-permute-start.5 = (bf16[64,1280]{1,0:T(8,128)(2,1)S(1)}, bf16[64,1280]{1,0:T(8,128)(2,1)S(1)}, u32[]{:S(2)}, u32[]{:S(2)}) collective-permute-start(bf16[64,1280]{1,0:T(8,128)(2,1)S(1)} %get-tuple-element.31), channel_id=1, source_target_pairs={{0,6},{1,7},{2,0},{3,1},{4,2},{5,3},{6,4},{7,5},{8,14},{9,15},{10,... | collective-permute-start | bytes 491528 | tf_op jit(solution)/shard_map/ppermute | solution.py:47
  22.0 12.1 %collective-permute-start.6 = (bf16[64,1280]{1,0:T(8,128)(2,1)S(1)}, bf16[64,1280]{1,0:T(8,128)(2,1)S(1)}, u32[]{:S(2)}, u32[]{:S(2)}) collective-permute-start(bf16[64,1280]{1,0:T(8,128)(2,1)S(1)} %get-tuple-element.33), channel_id=1, source_target_pairs={{0,8},{1,9},{2,10},{3,11},{4,12},{5,13},{6,14},{7,15},{8,16},{9,17... | collective-permute-start | bytes 491528 | tf_op jit(solution)/shard_map/ppermute | solution.py:51
  25.1 15.3 %collective-permute-start.7 = (bf16[64,1280]{1,0:T(8,128)(2,1)S(1)}, bf16[64,1280]{1,0:T(8,128)(2,1)S(1)}, u32[]{:S(2)}, u32[]{:S(2)}) collective-permute-start(bf16[64,1280]{1,0:T(8,128)(2,1)S(1)} %get-tuple-element.34), channel_id=1, source_target_pairs={{0,16},{1,17},{2,18},{3,19},{4,20},{5,21},{6,22},{7,23},{8,24},{9,... | collective-permute-start | bytes 491528 | tf_op jit(solution)/shard_map/ppermute | solution.py:51
  30.2 18.4 %collective-permute-start.8 = (bf16[64,1280]{1,0:T(8,128)(2,1)S(1)}, bf16[64,1280]{1,0:T(8,128)(2,1)S(1)}, u32[]{:S(2)}, u32[]{:S(2)}) collective-permute-start(bf16[64,1280]{1,0:T(8,128)(2,1)S(1)} %get-tuple-element.35), channel_id=1, source_target_pairs={{0,24},{1,25},{2,26},{3,27},{4,28},{5,29},{6,30},{7,31},{8,0},{9,1... | collective-permute-start | bytes 491528 | tf_op jit(solution)/shard_map/ppermute | solution.py:51
  51.3 63.1 %all-to-all-start = ((bf16[8,64,1280]{2,1,0:T(8,128)(2,1)}), bf16[8,64,1280]{2,1,0:T(8,128)(2,1)S(1)}, u32[]{:S(2)}, u32[]{:S(2)}) async-start(bf16[8,64,1280]{2,1,0:T(8,128)(2,1)} %bitcast.6), calls=%async_computation | async-start | bytes 2621440 | tf_op jit(solution)/shard_map/all_to_all | solution.py:343
  64.6 6.6 %collective-permute-start.16 = (bf16[80,480]{1,0:T(8,128)(2,1)S(1)}, bf16[80,480]{1,0:T(8,128)(2,1)S(1)}, u32[]{:S(2)}, u32[]{:S(2)}) collective-permute-start(bf16[80,480]{1,0:T(8,128)(2,1)S(1)} %get-tuple-element.47), channel_id=1, source_target_pairs={{0,2},{1,3},{2,4},{3,5},{4,6},{5,7},{6,0},{7,1},{8,10},{9,11},{10,... | collective-permute-start | bytes 230408 | tf_op jit(solution)/shard_map/ppermute | solution.py:47
  71.2 32.0 %collective-permute-start.19 = (bf16[320,480]{1,0:T(8,128)(2,1)S(1)}, bf16[320,480]{1,0:T(8,128)(2,1)S(1)}, u32[]{:S(2)}, u32[]{:S(2)}) collective-permute-start(bf16[320,480]{1,0:T(8,128)(2,1)S(1)} %pad_maximum_fusion.refs_4_), channel_id=1, source_target_pairs={{0,8},{1,9},{2,10},{3,11},{4,12},{5,13},{6,14},{7,15},{8,16},{9,17... | collective-permute-start | bytes 921608 | tf_op jit(solution)/shard_map/ppermute | solution.py:51
  75.1 38.7 %collective-permute-start.20 = (bf16[320,480]{1,0:T(8,128)(2,1)S(1)}, bf16[320,480]{1,0:T(8,128)(2,1)}, u32[]{:S(2)}, u32[]{:S(2)}) collective-permute-start(bf16[320,480]{1,0:T(8,128)(2,1)S(1)} %pad_maximum_fusion.refs_4_), channel_id=1, source_target_pairs={{0,16},{1,17},{2,18},{3,19},{4,20},{5,21},{6,22},{7,23},{8,24},{9,... | collective-permute-start | bytes 921608 | tf_op jit(solution)/shard_map/ppermute | solution.py:51
  75.9 37.9 %collective-permute-start.21 = (bf16[320,480]{1,0:T(8,128)(2,1)S(1)}, bf16[320,480]{1,0:T(8,128)(2,1)}, u32[]{:S(2)}, u32[]{:S(2)}) collective-permute-start(bf16[320,480]{1,0:T(8,128)(2,1)S(1)} %pad_maximum_fusion.refs_4_), channel_id=1, source_target_pairs={{0,24},{1,25},{2,26},{3,27},{4,28},{5,29},{6,30},{7,31},{8,0},{9,1... | collective-permute-start | bytes 921608 | tf_op jit(solution)/shard_map/ppermute | solution.py:51
  78.8 62.2 %collective-permute-start.22 = (bf16[320,480]{1,0:T(8,128)(2,1)S(1)}, bf16[320,480]{1,0:T(8,128)(2,1)}, u32[]{:S(2)}, u32[]{:S(2)}) collective-permute-start(bf16[320,480]{1,0:T(8,128)(2,1)S(1)} %pad_maximum_fusion.refs_4_), channel_id=1, source_target_pairs={{0,1},{1,0},{2,3},{3,2},{4,5},{5,4},{6,7},{7,6},{8,9},{9,8},{10,11... | collective-permute-start | bytes 921608 | tf_op jit(solution)/shard_map/ppermute | solution.py:55
  103.2 40.0 %collective-permute-start.23 = (bf16[320,480]{1,0:T(8,128)(2,1)S(1)}, bf16[320,480]{1,0:T(8,128)(2,1)}, u32[]{:S(2)}, u32[]{:S(2)}) collective-permute-start(bf16[320,480]{1,0:T(8,128)(2,1)S(1)} %collective-permute-done.19.refs_5_), channel_id=1, source_target_pairs={{0,1},{1,0},{2,3},{3,2},{4,5},{5,4},{6,7},{7,6},{8,9},{9,8},{10,11... | collective-permute-start | bytes 921608 | tf_op jit(solution)/shard_map/ppermute | solution.py:55
  113.8 30.4 %collective-permute-start.24 = (bf16[320,480]{1,0:T(8,128)(2,1)}, bf16[320,480]{1,0:T(8,128)(2,1)}, u32[]{:S(2)}, u32[]{:S(2)}) collective-permute-start(bf16[320,480]{1,0:T(8,128)(2,1)} %collective-permute-done.20.refs_6_), channel_id=1, source_target_pairs={{0,1},{1,0},{2,3},{3,2},{4,5},{5,4},{6,7},{7,6},{8,9},{9,8},{10,11... | collective-permute-start | bytes 921608 | tf_op jit(solution)/shard_map/ppermute | solution.py:55
  113.9 30.4 %collective-permute-start.25 = (bf16[320,480]{1,0:T(8,128)(2,1)}, bf16[320,480]{1,0:T(8,128)(2,1)}, u32[]{:S(2)}, u32[]{:S(2)}) collective-permute-start(bf16[320,480]{1,0:T(8,128)(2,1)} %collective-permute-done.21.refs_7_), channel_id=1, source_target_pairs={{0,1},{1,0},{2,3},{3,2},{4,5},{5,4},{6,7},{7,6},{8,9},{9,8},{10,11... | collective-permute-start | bytes 921608 | tf_op jit(solution)/shard_map/ppermute | solution.py:55
  117.8 10.5 %collective-permute-start.9 = (bf16[16,1280]{1,0:T(8,128)(2,1)}, bf16[16,1280]{1,0:T(8,128)(2,1)S(1)}, u32[]{:S(2)}, u32[]{:S(2)}) collective-permute-start(bf16[16,1280]{1,0:T(8,128)(2,1)} %get-tuple-element.37), channel_id=1, source_target_pairs={{0,8},{1,9},{2,10},{3,11},{4,12},{5,13},{6,14},{7,15},{8,16},{9,17... | collective-permute-start | bytes 122888 | tf_op jit(solution)/shard_map/ppermute | solution.py:51
  128.3 7.0 %collective-permute-start.10 = (bf16[16,1280]{1,0:T(8,128)(2,1)}, bf16[16,1280]{1,0:T(8,128)(2,1)S(1)}, u32[]{:S(2)}, u32[]{:S(2)}) collective-permute-start(bf16[16,1280]{1,0:T(8,128)(2,1)} %get-tuple-element.38), channel_id=1, source_target_pairs={{0,16},{1,17},{2,18},{3,19},{4,20},{5,21},{6,22},{7,23},{8,24},{9,... | collective-permute-start | bytes 122888 | tf_op jit(solution)/shard_map/ppermute | solution.py:51
  141.0 6.7 %collective-permute-start.13 = (bf16[64,1280]{1,0:T(8,128)(2,1)S(1)}, bf16[64,1280]{1,0:T(8,128)(2,1)S(1)}, u32[]{:S(2)}, u32[]{:S(2)}) collective-permute-start(bf16[64,1280]{1,0:T(8,128)(2,1)S(1)} %constant_dynamic-update-slice_fusion.refs_0_), channel_id=1, source_target_pairs={{0,4},{1,5},{2,6},{3,7},{4,0},{5,1},{6,2},{7,3},{8,12},{9,13},{10,... | collective-permute-start | bytes 491528 | tf_op jit(solution)/shard_map/ppermute | solution.py:47
  152.2 7.1 %collective-permute-start.26 = (bf16[256,320]{1,0:T(8,128)(2,1)S(1)}, bf16[256,320]{1,0:T(8,128)(2,1)S(1)}, u32[]{:S(2)}, u32[]{:S(2)}) collective-permute-start(bf16[256,320]{1,0:T(8,128)(2,1)S(1)} %shard_map.146.refs_4_), channel_id=1, source_target_pairs={{0,2},{1,3},{2,4},{3,5},{4,6},{5,7},{6,0},{7,1},{8,10},{9,11},{10,... | collective-permute-start | bytes 491528 | tf_op jit(solution)/shard_map/ppermute | solution.py:47
  153.4 7.1 %collective-permute-start.27 = (bf16[256,320]{1,0:T(8,128)(2,1)S(1)}, bf16[256,320]{1,0:T(8,128)(2,1)S(1)}, u32[]{:S(2)}, u32[]{:S(2)}) collective-permute-start(bf16[256,320]{1,0:T(8,128)(2,1)S(1)} %shard_map.146.refs_4_), channel_id=1, source_target_pairs={{0,4},{1,5},{2,6},{3,7},{4,0},{5,1},{6,2},{7,3},{8,12},{9,13},{10,... | collective-permute-start | bytes 491528 | tf_op jit(solution)/shard_map/ppermute | solution.py:47
  158.0 10.6 %collective-permute-start = (bf16[64,1024]{1,0:T(8,128)(2,1)S(1)}, bf16[64,1024]{1,0:T(8,128)(2,1)S(1)}, u32[]{:S(2)}, u32[]{:S(2)}) collective-permute-start(bf16[64,1024]{1,0:T(8,128)(2,1)S(1)} %get-tuple-element.25), channel_id=1, source_target_pairs={{0,2},{1,3},{2,4},{3,5},{4,6},{5,7},{6,0},{7,1},{8,10},{9,11},{10,... | collective-permute-start | bytes 393224 | tf_op jit(solution)/shard_map/ppermute | solution.py:47
  158.0 13.0 %collective-permute-start.1 = (bf16[64,1024]{1,0:T(8,128)(2,1)S(1)}, bf16[64,1024]{1,0:T(8,128)(2,1)S(1)}, u32[]{:S(2)}, u32[]{:S(2)}) collective-permute-start(bf16[64,1024]{1,0:T(8,128)(2,1)S(1)} %get-tuple-element.26), channel_id=1, source_target_pairs={{0,4},{1,5},{2,6},{3,7},{4,0},{5,1},{6,2},{7,3},{8,12},{9,13},{10,... | collective-permute-start | bytes 393224 | tf_op jit(solution)/shard_map/ppermute | solution.py:47
  163.7 15.8 %collective-permute-start.29 = (bf16[256,256]{1,0:T(8,128)(2,1)S(1)}, bf16[256,256]{1,0:T(8,128)(2,1)S(1)}, u32[]{:S(2)}, u32[]{:S(2)}) collective-permute-start(bf16[256,256]{1,0:T(8,128)(2,1)S(1)} %shard_map.147.refs_4_), channel_id=1, source_target_pairs={{0,8},{1,9},{2,10},{3,11},{4,12},{5,13},{6,14},{7,15},{8,16},{9,17... | collective-permute-start | bytes 393224 | tf_op jit(solution)/shard_map/ppermute | solution.py:51
  165.2 14.4 %collective-permute-start.30 = (bf16[256,256]{1,0:T(8,128)(2,1)S(1)}, bf16[256,256]{1,0:T(8,128)(2,1)S(1)}, u32[]{:S(2)}, u32[]{:S(2)}) collective-permute-start(bf16[256,256]{1,0:T(8,128)(2,1)S(1)} %shard_map.147.refs_4_), channel_id=1, source_target_pairs={{0,16},{1,17},{2,18},{3,19},{4,20},{5,21},{6,22},{7,23},{8,24},{9,... | collective-permute-start | bytes 393224 | tf_op jit(solution)/shard_map/ppermute | solution.py:51
  168.4 17.3 %collective-permute-start.31 = (bf16[256,256]{1,0:T(8,128)(2,1)S(1)}, bf16[256,256]{1,0:T(8,128)(2,1)S(1)}, u32[]{:S(2)}, u32[]{:S(2)}) collective-permute-start(bf16[256,256]{1,0:T(8,128)(2,1)S(1)} %shard_map.147.refs_4_), channel_id=1, source_target_pairs={{0,24},{1,25},{2,26},{3,27},{4,28},{5,29},{6,30},{7,31},{8,0},{9,1... | collective-permute-start | bytes 393224 | tf_op jit(solution)/shard_map/ppermute | solution.py:51
  168.6 17.1 %collective-permute-start.2 = (bf16[64,1024]{1,0:T(8,128)(2,1)S(1)}, bf16[64,1024]{1,0:T(8,128)(2,1)S(1)}, u32[]{:S(2)}, u32[]{:S(2)}) collective-permute-start(bf16[64,1024]{1,0:T(8,128)(2,1)S(1)} %get-tuple-element.27), channel_id=1, source_target_pairs={{0,6},{1,7},{2,0},{3,1},{4,2},{5,3},{6,4},{7,5},{8,14},{9,15},{10,... | collective-permute-start | bytes 393224 | tf_op jit(solution)/shard_map/ppermute | solution.py:47
  171.0 14.7 %collective-permute-start.32 = (bf16[256,256]{1,0:T(8,128)(2,1)S(1)}, bf16[256,256]{1,0:T(8,128)(2,1)S(1)}, u32[]{:S(2)}, u32[]{:S(2)}) collective-permute-start(bf16[256,256]{1,0:T(8,128)(2,1)S(1)} %shard_map.147.refs_4_), channel_id=1, source_target_pairs={{0,1},{1,0},{2,3},{3,2},{4,5},{5,4},{6,7},{7,6},{8,9},{9,8},{10,11... | collective-permute-start | bytes 393224 | tf_op jit(solution)/shard_map/ppermute | solution.py:55
  179.5 6.2 %collective-permute-start.33 = (bf16[256,256]{1,0:T(8,128)(2,1)S(1)}, bf16[256,256]{1,0:T(8,128)(2,1)S(1)}, u32[]{:S(2)}, u32[]{:S(2)}) collective-permute-start(bf16[256,256]{1,0:T(8,128)(2,1)S(1)} %collective-permute-done.29.refs_5_), channel_id=1, source_target_pairs={{0,1},{1,0},{2,3},{3,2},{4,5},{5,4},{6,7},{7,6},{8,9},{9,8},{10,11... | collective-permute-start | bytes 393224 | tf_op jit(solution)/shard_map/ppermute | solution.py:55
  179.6 7.1 %collective-permute-start.34 = (bf16[256,256]{1,0:T(8,128)(2,1)S(1)}, bf16[256,256]{1,0:T(8,128)(2,1)S(1)}, u32[]{:S(2)}, u32[]{:S(2)}) collective-permute-start(bf16[256,256]{1,0:T(8,128)(2,1)S(1)} %collective-permute-done.30.refs_6_), channel_id=1, source_target_pairs={{0,1},{1,0},{2,3},{3,2},{4,5},{5,4},{6,7},{7,6},{8,9},{9,8},{10,11... | collective-permute-start | bytes 393224 | tf_op jit(solution)/shard_map/ppermute | solution.py:55
  199.6 5.9 %collective-permute-start.37 = (bf16[64,1024]{1,0:T(8,128)(2,1)S(1)}, bf16[64,1024]{1,0:T(8,128)(2,1)S(1)}, u32[]{:S(2)}, u32[]{:S(2)}) collective-permute-start(bf16[64,1024]{1,0:T(8,128)(2,1)S(1)} %get-tuple-element.44), channel_id=1, source_target_pairs={{0,4},{1,5},{2,6},{3,7},{4,0},{5,1},{6,2},{7,3},{8,12},{9,13},{10,... | collective-permute-start | bytes 393224 | tf_op jit(solution)/shard_map/ppermute | solution.py:47
  201.3 7.6 %collective-permute-start.38 = (bf16[64,1024]{1,0:T(8,128)(2,1)S(1)}, bf16[64,1024]{1,0:T(8,128)(2,1)S(1)}, u32[]{:S(2)}, u32[]{:S(2)}) collective-permute-start(bf16[64,1024]{1,0:T(8,128)(2,1)S(1)} %get-tuple-element.45), channel_id=1, source_target_pairs={{0,2},{1,3},{2,4},{3,5},{4,6},{5,7},{6,0},{7,1},{8,10},{9,11},{10,... | collective-permute-start | bytes 393224 | tf_op jit(solution)/shard_map/ppermute | solution.py:47
  (25 other events, 490.1 us)
Sparse Core Ops, SparseCore 0:
  10.6 88.4 all-gather.1
